TPU v7x, 32 devices: a whole 2x2x4 slice. The times are simulated.
32 devices in a mesh: group: 2 (over y), box: 4 (over z), row: 2 (over x), freq: 2 (over core).
Axes of the slice: x: 2, y: 2, z: 4, core: 2. Of those that a mesh axis runs over, the one named last changes fastest.
Arguments:
- base_maps: float32 [16, 4, 2, 256, 256], P(('group', 'box'), 'freq'), parts along dimension 0, may hold values from -0.21875 to 0.21875
- lift_rows: float32 [16, 4, 2, 256, 256], P(('group', 'box'), 'freq', None, 'row'), parts along dimension 0, may hold values from -0.125 to 0.125
- probe_rows: float32 [16, 4, 2, 256, 256], P(('group', 'box'), 'freq', None, 'row'), parts along dimension 0, may hold values from -0.125 to 0.125
- wavenumber: float32 [8], P(('group', 'freq')), parts along dimension 0, may hold values from 0.7 to 1.4
- contrast: float32 [16, 256], P(('group', 'box'), 'row'), parts along dimension 0, may hold values from 0 to 1
- tree_order: int32 [16], P('group'), parts along dimension 0, may hold values from 0 to 7, each once
- illumination: float32 [2, 4, 2, 256, 32], P('group', 'freq'), parts along dimension 0, may hold values from -6 to 6
- observed: float32 [2, 4, 2, 256, 32], P('group', 'freq'), parts along dimension 0, may hold values from -3 to 3
Outputs:
- contrast_gradient: float32 [16, 256], P(('group', 'box'), 'row'), parts along dimension 0
There are 2 independent parts, one for each index of `group`. A program takes and returns all parts, laid end to end along the dimension named above; each array names one. Nothing has to cross between parts.
Inputs may be any that keep to these rules, and one draw needn't show every extreme that they name: tree_order is a permutation of the 8 stored rows.
All inputs are finite; a program needn't handle non-finite values.
Results may differ from a plain program's by a relative error of at most 0.0003.
Values sent between devices are 32-bit elements; how exact they have to be, the bound alone decides.
A program may use at most 64 MiB of HBM per device.

v0:
```python
from functools import partial

import jax
import jax.numpy as jnp
from jax import lax
from jax.sharding import PartitionSpec as P

LEVELS = 3


def from_partner(block, axis, apart):
    count = lax.axis_size(axis)
    route = []
    for low in range(count):
        high = low | 1 << apart
        if high != low and high < count:
            route += [(low, high), (high, low)]
    return lax.ppermute(block, axis, route)


def complex_mul(matrix_a, matrix_b):
    product = partial(jnp.matmul, precision=lax.Precision.HIGHEST)
    real_a, imag_a = (matrix_a[..., 0, :, :], matrix_a[..., 1, :, :])
    real_b, imag_b = (matrix_b[..., 0, :, :], matrix_b[..., 1, :, :])
    return jnp.stack(
        [
            product(real_a, real_b) - product(imag_a, imag_b),
            product(real_a, imag_b) + product(imag_a, real_b),
        ],
        axis=-3,
    )


def conj_transpose(matrix):
    return jnp.stack(
        [jnp.swapaxes(matrix[..., 0, :, :], -1, -2), -jnp.swapaxes(matrix[..., 1, :, :], -1, -2)],
        axis=-3,
    )


def approx_inverse(coupled):
    real_part = coupled[..., 0, :, :]
    unit = jnp.broadcast_to(jnp.eye(coupled.shape[-1], dtype=coupled.dtype), real_part.shape)
    identity = jnp.stack([unit, jnp.zeros_like(real_part)], axis=-3)
    system = identity - coupled
    iterate = identity + coupled
    iterate = complex_mul(iterate, 2.0 * identity - complex_mul(system, iterate))
    return iterate


def split_blocks(matrix, half):
    return (
        matrix[..., :half, :half],
        matrix[..., :half, half:],
        matrix[..., half:, :half],
        matrix[..., half:, half:],
    )


def merge_pair(west, east):
    half = west.shape[-1] // 2
    west_outer, west_cross, west_enter, west_inner = split_blocks(west, half)
    east_outer, east_cross, east_enter, east_inner = split_blocks(east, half)
    forward_inv = approx_inverse(complex_mul(east_inner, west_inner))
    backward_inv = approx_inverse(complex_mul(west_inner, east_inner))
    reach_west = complex_mul(forward_inv, complex_mul(east_inner, west_enter))
    reach_east = complex_mul(forward_inv, east_enter)
    echo_west = west_enter + complex_mul(west_inner, reach_west)
    echo_east = complex_mul(west_inner, reach_east)
    top_rows = jnp.concatenate(
        [west_outer + complex_mul(west_cross, reach_west), complex_mul(west_cross, reach_east)],
        axis=-1,
    )
    bottom_rows = jnp.concatenate(
        [complex_mul(east_cross, echo_west), east_outer + complex_mul(east_cross, echo_east)],
        axis=-1,
    )
    return (jnp.concatenate([top_rows, bottom_rows], axis=-2), forward_inv, backward_inv)


def descend_pair(west, east, forward_inv, backward_inv, incoming, adjoint):
    half = west.shape[-1] // 2
    west_outer, west_cross, west_enter, west_inner = split_blocks(west, half)
    east_outer, east_cross, east_enter, east_inner = split_blocks(east, half)
    given_west, given_east = (incoming[..., :half, :], incoming[..., half:, :])
    back_west, back_east = (adjoint[..., :half, :], adjoint[..., half:, :])
    into_west = complex_mul(west_enter, given_west)
    west_in = complex_mul(
        forward_inv, complex_mul(east_inner, into_west) + complex_mul(east_enter, given_east)
    )
    east_in = into_west + complex_mul(west_inner, west_in)
    crossed = complex_mul(conj_transpose(west_cross), back_west)
    west_back = complex_mul(
        conj_transpose(backward_inv),
        complex_mul(conj_transpose(east_inner), crossed)
        + complex_mul(conj_transpose(east_cross), back_east),
    )
    east_back = crossed + complex_mul(conj_transpose(west_inner), west_back)
    west_side = (
        jnp.concatenate([given_west, west_in], axis=-2),
        jnp.concatenate([back_west, west_back], axis=-2),
    )
    east_side = (
        jnp.concatenate([given_east, east_in], axis=-2),
        jnp.concatenate([back_east, east_back], axis=-2),
    )
    return (west_side, east_side)


def alternate(west, east):
    stacked = jnp.stack([west, east], axis=1)
    return stacked.reshape((-1,) + west.shape[1:])


def body(
    base_maps, lift_rows, probe_rows, wavenumber, contrast, tree_order, illumination, observed
):
    highest = lax.Precision.HIGHEST
    leaf_count = contrast.shape[0]
    tree_depth = leaf_count.bit_length() - 1
    box_index = lax.axis_index("box")
    positions = box_index * leaf_count + jnp.arange(leaf_count, dtype=jnp.int32)
    mine_order = jnp.take(tree_order, positions)
    every_contrast = lax.all_gather(contrast, "box", axis=0, tiled=True)
    selector = (
        mine_order[:, None] == jnp.arange(every_contrast.shape[0], dtype=jnp.int32)[None, :]
    ).astype(jnp.float32)
    tree_contrast = jnp.matmul(selector, every_contrast, precision=highest)
    squared = wavenumber * wavenumber
    weighted = (
        tree_contrast[:, None, None, :, None] * probe_rows * squared[None, :, None, None, None]
    )
    lift_swapped = jnp.swapaxes(lift_rows, -1, -2)
    node_maps = base_maps + lax.psum(complex_mul(lift_swapped, weighted), "row")
    saved = []
    whole_map = node_maps
    for level in range(LEVELS):
        if node_maps.shape[0] >= 2:
            former = node_maps[0::2]
            latter = node_maps[1::2]
            side_flag = None
        else:
            bit_index = level - tree_depth
            sibling = from_partner(node_maps, "box", bit_index)
            side_flag = box_index // 2**bit_index % 2
            former = jnp.where(side_flag == 0, node_maps, sibling)
            latter = jnp.where(side_flag == 0, sibling, node_maps)
        whole_map, forward_inv, backward_inv = merge_pair(former, latter)
        saved.append((former, latter, forward_inv, backward_inv, side_flag))
        node_maps = whole_map
    top_index = box_index * leaf_count // 8
    incoming = lax.dynamic_slice_in_dim(illumination, top_index, 1, 0)
    target = lax.dynamic_slice_in_dim(observed, top_index, 1, 0)
    adjoint = complex_mul(whole_map, incoming) - target
    for former, latter, forward_inv, backward_inv, side_flag in reversed(saved):
        west_side, east_side = descend_pair(
            former, latter, forward_inv, backward_inv, incoming, adjoint
        )
        if side_flag is None:
            incoming = alternate(west_side[0], east_side[0])
            adjoint = alternate(west_side[1], east_side[1])
        else:
            incoming = jnp.where(side_flag == 0, west_side[0], east_side[0])
            adjoint = jnp.where(side_flag == 0, west_side[1], east_side[1])
    conj_adjoint = jnp.stack([adjoint[..., 0, :, :], -adjoint[..., 1, :, :]], axis=-3)
    lifted = complex_mul(lift_rows, conj_adjoint)
    probed = complex_mul(probe_rows, incoming)
    contrib = lifted[:, :, 0] * probed[:, :, 0] - lifted[:, :, 1] * probed[:, :, 1]
    partial_grad = jnp.einsum("lfks,f->lk", contrib, squared, precision=highest)
    total = lax.psum(partial_grad, "freq")
    rows_here = jnp.arange(lax.axis_size("box") * leaf_count, dtype=jnp.int32)
    chooser = (rows_here[:, None] == mine_order[None, :]).astype(jnp.float32)
    return lax.psum_scatter(
        jnp.matmul(chooser, total, precision=highest), "box", scatter_dimension=0, tiled=True
    )


def solution(mesh):
    return jax.shard_map(
        body,
        mesh=mesh,
        in_specs=(
            P(("group", "box"), "freq", None, None, None),
            P(("group", "box"), "freq", None, "row", None),
            P(("group", "box"), "freq", None, "row", None),
            P(("group", "freq")),
            P(("group", "box"), "row"),
            P("group"),
            P("group", "freq", None, None, None),
            P("group", "freq", None, None, None),
        ),
        out_specs=P(("group", "box"), "row"),
        check_vma=False,
    )
```

profile of v0, /device:TPU:0, one launch (start us, length us, event | category | flops | bytes accessed | tf_op | source)
XLA Modules:
  0.0 296.2 jit_solution(2243450166303676634)
XLA Ops:
  6.5 0.8 mul.42
  7.3 0.6 gather_fusion
  8.0 12.8 %all-gather = f32[4,2,128]{2,1,0:T(2,128)S(1)} all-gather(f32[1,2,128]{2,1,0:T(2,128)} %bitcast.1537), channel_id=1, replica_groups=mesh['group'=2,'box'=4,'row'=2,'freq'=2] {'box'}, dimensions={0}, use_global_device_ids=true | all-gather | bytes 5120 | tf_op jit(solution)/shard_map/all_gather | solution.py:124
  20.8 1.5 copy.570
  22.4 1.3 copy.569
  23.9 1.4 multiply_multiply_fusion
  25.3 1.0 fusion.126
  26.2 1.0 fusion.125
  27.2 1.0 fusion
  28.3 1.0 fusion.1
  29.3 1.5 pad_maximum_fusion
  30.9 1.6 copy-done.13
  32.4 2.0 copy.571
  34.4 57.7 %all-reduce.4.cloned.1.call-done = f32[2,2,2,256,256]{3,4,1,0,2:T(8,128)} async-done(((f32[2,2,2,256,256]{3,4,1,0,2:T(8,128)}), f32[2,2,2,256,256]{3,4,1,0,2:T(8,128)}) %all-reduce.4.cloned.1.call-update) | async-done | bytes 2097168 | tf_op jit(solution)/shard_map/psum | solution.py:134
  92.1 2.6 add.580
  99.8 0.8 pad_add_fusion
  111.1 0.6 fusion.60
  114.6 1.0 maximum_maximum_fusion
  115.6 1.5 collective-permute-start
  117.1 0.6 dynamic-slice
  118.4 1.0 fusion.757
  119.4 1.2 fusion.452
  120.6 1.2 fusion.5
  121.8 1.2 fusion.453
  122.9 1.2 fusion.6
  124.1 16.7 %collective-permute-done = f32[1,2,2,256,256]{3,4,1,0,2:T(8,128)} collective-permute-done((f32[1,2,2,256,256]{3,4,1,0,2:T(8,128)}, f32[1,2,2,256,256]{3,4,1,0,2:T(8,128)}, u32[]{:S(2)}, u32[]{:S(2)}) %collective-permute-start) | collective-permute-done | bytes 1048608 | tf_op jit(solution)/shard_map/ppermute | solution.py:18
  140.8 1.4 broadcast_select_fusion.1
  153.8 0.8 convolution_subtract_fusion.30
  163.5 2.5 collective-permute-start.1
  167.4 43.6 %collective-permute-done.1 = f32[1,2,2,256,256]{3,4,1,0,2:T(8,128)S(1)} collective-permute-done((f32[1,2,2,256,256]{3,4,1,0,2:T(8,128)S(1)}, f32[1,2,2,256,256]{3,4,1,0,2:T(8,128)S(1)}, u32[]{:S(2)}, u32[]{:S(2)}) %collective-permute-start.1) | collective-permute-done | bytes 1048608 | tf_op jit(solution)/shard_map/ppermute | solution.py:18
  216.2 0.4 fusion.440
  228.2 0.4 convolution_subtract_fusion.15
  235.2 0.6 fusion.28
  240.3 0.4 fusion.127
  240.8 0.4 fusion.128
  241.2 0.4 fusion.68
  241.6 0.4 fusion.69
  267.2 0.6 fusion.115
  267.8 0.6 fusion.117
  270.3 0.6 fusion.121
  270.9 0.6 fusion.123
  271.5 0.6 convolution_add_fusion.47
  272.1 0.6 convolution_subtract_fusion.47
  272.7 0.6 fusion.67
  273.3 0.6 fusion.70
  274.1 2.5 psum.15
  276.7 11.6 %all-reduce.1 = f32[8,128]{1,0:T(8,128)S(1)} all-reduce(f32[8,128]{1,0:T(8,128)S(1)} %fusion.745), channel_id=2, replica_groups=mesh['group'=2,'box'=4,'row'=2,'freq'=2] {'box'}, use_global_device_ids=true, to_apply=%region_3.4.clone | all-reduce | flops 1024 | bytes 8192
  288.3 0.6 constant_dynamic-slice_fusion
  (390 shorter events, 94.1 us)
Async XLA Ops:
  6.5 0.8 copy-start
  6.5 15.8 %copy-start.3 = (f32[2,2,2,128,256]{4,3,2,1,0:T(8,128)S(1)}, f32[2,2,2,128,256]{4,3,2,1,0:T(8,128)}, u32[]{:S(2)}) copy-start(f32[2,2,2,128,256]{4,3,2,1,0:T(8,128)} %param.10) | copy-start | bytes 3145732
  6.5 85.6 %all-reduce.4.cloned.1.call-start = ((), (), s32[]{:S(2)}) async-start(), calls=%async_computation | async-start | bytes 4194304 | tf_op jit(solution)/shard_map/psum | solution.py:134
  30.8 1.6 copy-start.13
  97.9 2.7 copy-start.6
  101.4 5.8 %copy-start.4 = (f32[2,128,128]{2,1,0:T(8,128)}, f32[2,128,128]{2,1,0:T(8,128)S(1)}, u32[]{:S(2)}) copy-start(f32[2,128,128]{2,1,0:T(8,128)S(1)} %convolution_add_fusion.43) | copy-start | bytes 393220
  112.6 3.0 %copy-start.9 = (f32[1,2,2,128,128]{3,4,1,0,2:T(8,128)}, f32[1,2,2,128,128]{3,4,1,0,2:T(8,128)S(1)}, u32[]{:S(2)}) copy-start(f32[1,2,2,128,128]{3,4,1,0,2:T(8,128)S(1)} %get-tuple-element.9) | copy-start | bytes 786436
  112.6 3.0 %copy-start.11 = (f32[1,2,2,128,128]{3,4,1,0,2:T(8,128)}, f32[1,2,2,128,128]{3,4,1,0,2:T(8,128)S(1)}, u32[]{:S(2)}) copy-start(f32[1,2,2,128,128]{3,4,1,0,2:T(8,128)S(1)} %get-tuple-element.10) | copy-start | bytes 786436
  113.2 4.0 %copy-start.24 = (u32[32]{0:T(128)S(1)}, u32[32]{0:T(128)}, u32[]{:S(2)}) copy-start(u32[32]{0:T(128)} %constant.81) | copy-start | bytes 388
  113.6 3.5 %copy-start.14 = (f32[1,2,1,128,128]{3,4,1,0,2:T(8,128)}, f32[1,2,1,128,128]{3,4,1,0,2:T(8,128)S(1)}, u32[]{:S(2)}) copy-start(f32[1,2,1,128,128]{3,4,1,0,2:T(8,128)S(1)} %fusion.57) | copy-start | bytes 393220
  114.0 3.1 %copy-start.16 = (f32[1,2,1,128,128]{3,4,1,0,2:T(8,128)}, f32[1,2,1,128,128]{3,4,1,0,2:T(8,128)S(1)}, u32[]{:S(2)}) copy-start(f32[1,2,1,128,128]{3,4,1,0,2:T(8,128)S(1)} %fusion.58) | copy-start | bytes 393220
  114.3 2.8 copy-start.18
  114.5 2.5 copy-start.20
  115.6 25.2 %collective-permute-start = (f32[1,2,2,256,256]{3,4,1,0,2:T(8,128)}, f32[1,2,2,256,256]{3,4,1,0,2:T(8,128)}, u32[]{:S(2)}, u32[]{:S(2)}) collective-permute-start(f32[1,2,2,256,256]{3,4,1,0,2:T(8,128)} %maximum_maximum_fusion), channel_id=1, source_target_pairs={{0,4},{4,0},{8,12},{12,8},{1,5},{5,1},{9,13},{13,9},{2,6},{6,2},{1... | collective-permute-start | bytes 3145736 | tf_op jit(solution)/shard_map/ppermute | solution.py:18
  118.4 22.4 %copy-start.10 = (f32[1,2,2,128,128]{3,4,1,0,2:T(8,128)S(1)}, f32[1,2,2,128,128]{3,4,1,0,2:T(8,128)}, u32[]{:S(2)}) copy-start(f32[1,2,2,128,128]{3,4,1,0,2:T(8,128)} %copy-done.9) | copy-start | bytes 786436
  118.4 22.4 %copy-start.12 = (f32[1,2,2,128,128]{3,4,1,0,2:T(8,128)S(1)}, f32[1,2,2,128,128]{3,4,1,0,2:T(8,128)}, u32[]{:S(2)}) copy-start(f32[1,2,2,128,128]{3,4,1,0,2:T(8,128)} %copy-done.11) | copy-start | bytes 786436
  118.4 22.4 %copy-start.15 = (f32[1,2,1,128,128]{3,4,1,0,2:T(8,128)S(1)}, f32[1,2,1,128,128]{3,4,1,0,2:T(8,128)}, u32[]{:S(2)}) copy-start(f32[1,2,1,128,128]{3,4,1,0,2:T(8,128)} %copy-done.14) | copy-start | bytes 393220
  118.4 22.4 %copy-start.17 = (f32[1,2,1,128,128]{3,4,1,0,2:T(8,128)S(1)}, f32[1,2,1,128,128]{3,4,1,0,2:T(8,128)}, u32[]{:S(2)}) copy-start(f32[1,2,1,128,128]{3,4,1,0,2:T(8,128)} %copy-done.16) | copy-start | bytes 393220
  118.4 22.4 %copy-start.19 = (f32[1,2,1,128,128]{3,4,1,0,2:T(8,128)S(1)}, f32[1,2,1,128,128]{3,4,1,0,2:T(8,128)}, u32[]{:S(2)}) copy-start(f32[1,2,1,128,128]{3,4,1,0,2:T(8,128)} %copy-done.18) | copy-start | bytes 393220
  118.4 22.4 %copy-start.21 = (f32[1,2,1,128,128]{3,4,1,0,2:T(8,128)S(1)}, f32[1,2,1,128,128]{3,4,1,0,2:T(8,128)}, u32[]{:S(2)}) copy-start(f32[1,2,1,128,128]{3,4,1,0,2:T(8,128)} %copy-done.20) | copy-start | bytes 393220
  142.7 3.6 %copy-start.7 = (f32[1,2,1,128,128]{4,3,1,2,0:T(8,128)S(1)}, f32[1,2,1,128,128]{4,3,1,2,0:T(8,128)}, u32[]{:S(2)}) copy-start(f32[1,2,1,128,128]{4,3,1,2,0:T(8,128)} %copy-done.6) | copy-start | bytes 393220
  163.5 47.5 %collective-permute-start.1 = (f32[1,2,2,256,256]{3,4,1,0,2:T(8,128)S(1)}, f32[1,2,2,256,256]{3,4,1,0,2:T(8,128)S(1)}, u32[]{:S(2)}, u32[]{:S(2)}) collective-permute-start(f32[1,2,2,256,256]{3,4,1,0,2:T(8,128)S(1)} %maximum_maximum_fusion.1), channel_id=1, source_target_pairs={{0,8},{8,0},{4,12},{12,4},{1,9},{9,1},{5,13},{13,5},{2,10},{10,2},... | collective-permute-start | bytes 3145736 | tf_op jit(solution)/shard_map/ppermute | solution.py:18
  167.4 43.8 %copy-start.8 = (f32[1,2,2,256,32]{3,4,2,1,0:T(8,128)S(1)}, f32[1,2,2,256,32]{3,4,2,1,0:T(8,128)}, u32[]{:S(2)}) copy-start(f32[1,2,2,256,32]{3,4,2,1,0:T(8,128)} %param.14) | copy-start | bytes 393220
  240.2 1.9 copy-start.22
  261.2 4.3 %copy-start.5 = (f32[2,128,128]{2,1,0:T(8,128)S(1)}, f32[2,128,128]{2,1,0:T(8,128)}, u32[]{:S(2)}) copy-start(f32[2,128,128]{2,1,0:T(8,128)} %copy-done.4) | copy-start | bytes 393220
  267.2 3.1 %copy-start.2 = (f32[2,2,2,128,256]{4,3,2,1,0:T(8,128)S(1)}, f32[2,2,2,128,256]{4,3,2,1,0:T(8,128)}, u32[]{:S(2)}) copy-start(f32[2,2,2,128,256]{4,3,2,1,0:T(8,128)} %param.9) | copy-start | bytes 3145732
  270.3 18.6 %copy-start.1 = (s32[8]{0:T(128)S(1)}, s32[8]{0:T(128)}, u32[]{:S(2)}) copy-start(s32[8]{0:T(128)} %param.13) | copy-start | bytes 100
  270.9 3.0 %copy-start.23 = (f32[2]{0:T(128)S(1)}, f32[2]{0:T(128)}, u32[]{:S(2)}) copy-start(f32[2]{0:T(128)} %param.11) | copy-start | bytes 28
Sparse Core Ops, SparseCore 0:
  31.0 61.1 all-reduce.3
where the time goes:
time: 301 us; the launch traced here: 296 us
  waiting for transfers between devices  118 us (39%)
  matrix products  110 us (37%)
  blocking collectives  26.9 us (9%)
  between operations  16.5 us (5%)
  other arithmetic  11.1 us (4%)
  local copies, waits for them, and re-layouts  9.36 us (3%)
  starting transfers between devices  3.96 us (1%)
    ppermute x2, waiting for transfers between devices, from_partner(): return lax.ppermute(block, axis, route)  60.3 us
    psum x1, waiting for transfers between devices, body(): node_maps = base_maps + lax.psum(complex_mul(lift_swapped, weighted), 'row')  57.7 us
    dot_general x79, matrix products, complex_mul(): product(real_a, real_b) - product(imag_a, imag_b)  27.8 us
    dot_general x79, matrix products, complex_mul(): product(imag_a, imag_b)  27.5 us
    dot_general x79, matrix products, complex_mul(): product(imag_a, real_b)  27.3 us
    dot_general x79, matrix products, complex_mul(): product(real_a, imag_b) + product(imag_a, real_b)  27.3 us
    all_gather x1, blocking collectives, body(): every_contrast = lax.all_gather(contrast, 'box', axis=0, tiled=True)  12.8 us
    unnamed x1, blocking collectives  11.6 us
  transfers between devices with their start and end apart: 3, of which 3 were waited for; matrix products, arithmetic and copies ran while one was open for 3% of the time, Pallas kernels for 0%

commit v1 on v0

--- a/solution.py
+++ b/solution.py
@@ -3,6 +3,8 @@
 import jax
 import jax.numpy as jnp
 from jax import lax
+from jax.experimental import pallas as pl
+from jax.experimental.pallas import tpu as pltpu
 from jax.sharding import PartitionSpec as P
 
 LEVELS = 3
@@ -175,9 +177,424 @@
     )
 
 
+H = 128
+MESH = pl.DeviceIdType.MESH
+F32 = jnp.float32
+
+
+def halves(x):
+    high = x.astype(jnp.bfloat16)
+    return high, (x - high.astype(F32)).astype(jnp.bfloat16)
+
+
+def mm(a, b):
+    dot = partial(jnp.dot, preferred_element_type=F32)
+    return dot(a[0], b[0]) + (dot(a[0], b[1]) + dot(a[1], b[0]))
+
+
+def blk(x):
+    turned = jnp.concatenate([-x[H:], x[:H]], axis=0)
+    return jnp.concatenate([x, turned], axis=1)
+
+
+def apply_iterate(op, x):
+    once = mm(op, halves(x))
+    even = x + mm(op, halves(once))
+    return even + mm(op, halves(even))
+
+
+def pack(x):
+    q = x.shape[0] // 4
+    return jnp.concatenate([x[i * q : (i + 1) * q] for i in range(4)], axis=1)
+
+
+def unpack(x):
+    q = x.shape[1] // 4
+    return jnp.concatenate([x[:, i * q : (i + 1) * q] for i in range(4)], axis=0)
+
+
+def adjoint_maps(a13, a33, b23, b33):
+    op_a33, op_a13, op_b23 = halves(blk(a33)), halves(blk(a13)), halves(blk(b23))
+    split_b33, split_a33 = halves(b33), halves(a33)
+    coupled = mm(op_a33, split_b33)
+    op = halves(blk(coupled))
+    row = lax.broadcasted_iota(jnp.int32, (2 * H, H), 0)
+    col = lax.broadcasted_iota(jnp.int32, (2 * H, H), 1)
+    even = jnp.where(row == col, 1.0, 0.0) + mm(op, halves(coupled))
+    inverse = halves(even + mm(op, halves(even)))
+    f1 = blk(mm(halves(blk(mm(op_a13, split_b33))), inverse))
+    f2 = blk(mm(op_b23, inverse))
+    g1 = blk(a13 + mm(halves(f1), split_a33))
+    g2 = blk(mm(halves(f2), split_a33))
+    to_l3 = jnp.concatenate([f1.T, f2.T], axis=1)
+    to_k3 = jnp.concatenate([g1.T, g2.T], axis=1)
+    return to_l3, to_k3
+
+
+def incoming_maps(op_a33, op, b33a31, a31, b32):
+    reach = apply_iterate(op, jnp.concatenate([b33a31, b32], axis=1))
+    echo = mm(op_a33, halves(reach))
+    return reach, jnp.concatenate([echo[:, :H] + a31, echo[:, H:]], axis=1)
+
+
+def wide(x):
+    return jnp.concatenate([blk(x[:, :H]), blk(x[:, H:])], axis=1)
+
+
+def store_halves(ref, x):
+    high, low = halves(x)
+    ref[0] = high
+    ref[1] = low
+
+
+def load_halves(ref):
+    return ref[0], ref[1]
+
+
+def kernel(
+    base, lift, probe, wave, contrast, order, illum, observed, out,
+    lbuf, pbuf, bbuf, cbuf, own, got, t33, tvec, mbuf, vbuf, inc1, adj1, inc2, adj2,
+    gpart, grecv, gtot, loc_sem, xs_sem, xr_sem, cs_sem, cr_sem, zs_sem, zr_sem,
+    ts_sem, tr_sem, us_sem, ur_sem, ms_sem, mr_sem, vs_sem, vr_sem, gs_sem, gr_sem, hs_sem, hr_sem,
+):
+    box = lax.axis_index("box")
+    row = lax.axis_index("row")
+    core = lax.axis_index("freq")
+    side = lax.rem(box, 2)
+    pair = box // 2
+    mate = box + 1 - 2 * side
+    other = 1 - row
+    boxes = [lax.rem(box + d, 4) for d in (1, 2, 3)]
+    peers = [{"row": other, "freq": core}, {"row": row, "freq": 1 - core}, {"row": other, "freq": 1 - core}]
+
+    def remote(source, target, sender, receiver, where):
+        return pltpu.make_async_remote_copy(
+            src_ref=source, dst_ref=target, send_sem=sender, recv_sem=receiver,
+            device_id=where, device_id_type=MESH,
+        )
+
+    mine = pl.ds(pl.multiple_of(row * H, H), H)
+    theirs = pl.ds(pl.multiple_of(other * H, H), H)
+    loads = []
+    for leaf in range(2):
+        loads += [
+            (lift.at[leaf, row], lbuf.at[leaf, :, mine, :]),
+            (probe.at[leaf, row], pbuf.at[leaf, :, mine, :]),
+            (base.at[leaf, row], bbuf.at[leaf]),
+        ]
+    loads = [pltpu.make_async_copy(s, t, loc_sem.at[i]) for i, (s, t) in enumerate(loads)]
+    for load in loads:
+        load.start()
+
+    barrier = pltpu.get_barrier_semaphore()
+    for where in peers + [{"box": b} for b in boxes]:
+        pl.semaphore_signal(barrier, inc=1, device_id=where, device_id_type=MESH)
+    pl.semaphore_wait(barrier, 6)
+
+    cbuf[box, row] = contrast[...]
+    ahead = remote(contrast, cbuf.at[box, row], xs_sem.at[8], xr_sem.at[8], peers[0])
+    ahead.start()
+    low, high = pl.ds(0, H), pl.ds(H, H)
+    plan = [(lift, lbuf, 0, high), (probe, pbuf, 0, high), (lift, lbuf, 1, high), (probe, pbuf, 1, high)]
+    plan += [(probe, pbuf, 0, low), (probe, pbuf, 1, low), (lift, lbuf, 0, low), (lift, lbuf, 1, low)]
+    sends, waits = [ahead], []
+    for i, (source, target, leaf, cols) in enumerate(plan):
+        copy = remote(
+            source.at[leaf, other, :, :, cols], target.at[leaf, :, mine, cols],
+            xs_sem.at[i], xr_sem.at[i], peers[0],
+        )
+        copy.start()
+        sends.append(copy)
+        waits.append(
+            remote(
+                source.at[leaf, other, :, :, cols], target.at[leaf, :, theirs, cols],
+                xs_sem.at[i], xr_sem.at[i], peers[0],
+            )
+        )
+
+    remote(contrast, cbuf.at[box, other], xs_sem.at[8], xr_sem.at[8], peers[0]).wait_recv()
+    for d in range(3):
+        copy = remote(cbuf.at[box], cbuf.at[box], cs_sem.at[d], cr_sem.at[box], {"box": boxes[d]})
+        copy.start()
+        sends.append(copy)
+    for d in range(3):
+        slot = cbuf.at[boxes[d]]
+        remote(slot, slot, cs_sem.at[d], cr_sem.at[boxes[d]], {"box": boxes[d]}).wait_recv()
+    number = wave[row]
+    squared = number * number
+    weight = []
+    for leaf in range(2):
+        stored = order[box * 2 + leaf]
+        total = jnp.zeros((2, H), F32)
+        for j in range(8):
+            total = total + jnp.where(stored == j, cbuf[j // 2, :, j % 2, :], 0.0)
+        total = total * squared
+        weight.append(
+            jnp.concatenate([jnp.broadcast_to(total[i : i + 1], (H, H)).T for i in range(2)], axis=0)
+        )
+
+    for load in loads:
+        load.wait()
+    for copy in waits[:4]:
+        copy.wait_recv()
+
+    def lift_op(leaf, cols):
+        real, imag = lbuf[leaf, 0, :, cols].T, lbuf[leaf, 1, :, cols].T
+        upper = jnp.concatenate([real, -imag], axis=1)
+        return halves(jnp.concatenate([upper, jnp.concatenate([imag, real], axis=1)], axis=0))
+
+    def weighted(leaf, cols):
+        both = [pbuf[leaf, part, :, cols] * weight[leaf] for part in range(2)]
+        return halves(jnp.concatenate(both, axis=0))
+
+    def based(leaf, rows, cols):
+        return jnp.concatenate([bbuf[leaf, 0, rows, cols], bbuf[leaf, 1, rows, cols]], axis=0)
+
+    op3 = [lift_op(leaf, high) for leaf in range(2)]
+    w3 = [weighted(leaf, high) for leaf in range(2)]
+    a33, b33 = [based(leaf, high, high) + mm(op3[leaf], w3[leaf]) for leaf in range(2)]
+    op_a33, op_b33 = halves(blk(a33)), halves(blk(b33))
+    op = halves(blk(mm(op_b33, halves(a33))))
+    for copy in waits[4:6]:
+        copy.wait_recv()
+    w1 = [weighted(leaf, low) for leaf in range(2)]
+    a31, b32 = [based(leaf, high, low) + mm(op3[leaf], w1[leaf]) for leaf in range(2)]
+    reach, echo = incoming_maps(op_a33, op, mm(op_b33, halves(a31)), a31, b32)
+    for copy in waits[6:]:
+        copy.wait_recv()
+    op1 = [lift_op(leaf, low) for leaf in range(2)]
+    a13, b23 = [based(leaf, low, high) + mm(op1[leaf], w3[leaf]) for leaf in range(2)]
+    a11, b22 = [based(leaf, low, low) + mm(op1[leaf], w1[leaf]) for leaf in range(2)]
+    bottom = mm(halves(blk(b23)), halves(echo))
+    top = mm(halves(blk(a13)), halves(reach))
+    top_left, top_right = top[:, :H] + a11, top[:, H:]
+    low_left, low_right = bottom[:, :H], bottom[:, H:] + b22
+    own[0] = low_right
+    own[1] = low_left
+    own[2] = top_right
+    for i in range(3):
+        copy = remote(own.at[i], got.at[i], zs_sem.at[i], zr_sem.at[i], {"box": mate})
+        copy.start()
+        sends.append(copy)
+    store_halves(inc1.at[0], wide(reach))
+    store_halves(inc1.at[1], wide(echo))
+    to_l3, to_k3 = adjoint_maps(a13, a33, b23, b33)
+    store_halves(adj1.at[0], to_l3)
+    store_halves(adj1.at[1], to_k3)
+
+    def illum_half(ref, part):
+        rows = pl.ds(part * H, H)
+        return jnp.concatenate([ref[0, row, 0, rows, :], ref[0, row, 1, rows, :]], axis=0)
+
+    i1, j2 = illum_half(illum, 0), illum_half(illum, 1)
+    upper_pair = pair == 1
+    east = side == 1
+    given = jnp.where(upper_pair, j2, i1)
+
+    for i in range(2):
+        remote(own.at[i], got.at[i], zs_sem.at[i], zr_sem.at[i], {"box": mate}).wait_recv()
+    a33, b33 = jnp.where(east, got[0], low_right), jnp.where(east, low_right, got[0])
+    a31, b32 = jnp.where(east, got[1], low_left), jnp.where(east, low_left, got[1])
+    op_a33, op_b33 = halves(blk(a33)), halves(blk(b33))
+    op = halves(blk(mm(op_b33, halves(a33))))
+    reach, echo = incoming_maps(op_a33, op, mm(op_b33, halves(a31)), a31, b32)
+    half_map = mm(halves(blk(top_right)), halves(jnp.where(east, echo, reach)))
+    left = half_map[:, :H] + jnp.where(east, 0.0, top_left)
+    right = half_map[:, H:] + jnp.where(east, top_left, 0.0)
+    op_left, op_right = halves(blk(left)), halves(blk(right))
+
+    @pl.when(east)
+    def _():
+        t33[pair] = right
+        tvec[pair] = pack(mm(op_left, halves(given)))
+        for d in range(3):
+            where = {"box": boxes[d]}
+            remote(t33.at[pair], t33.at[pair], ts_sem.at[d], tr_sem.at[pair], where).start()
+            remote(tvec.at[pair], tvec.at[pair], us_sem.at[d], ur_sem.at[pair], where).start()
+
+    store_halves(inc2, wide(jnp.where(east, echo, reach)))
+    remote(own.at[2], got.at[2], zs_sem.at[2], zr_sem.at[2], {"box": mate}).wait_recv()
+    a13, b23 = jnp.where(east, got[2], top_right), jnp.where(east, top_right, got[2])
+    to_l3, to_k3 = adjoint_maps(a13, a33, b23, b33)
+    store_halves(adj2, jnp.where(east, to_k3, to_l3))
+    op_right_t = halves(blk(right).T)
+
+    for s in range(2):
+
+        @pl.when(box != 2 * s + 1)
+        def _():
+            where = {"box": boxes[0]}
+            remote(t33.at[s], t33.at[s], ts_sem.at[0], tr_sem.at[s], where).wait_recv()
+            remote(tvec.at[s], tvec.at[s], us_sem.at[0], ur_sem.at[s], where).wait_recv()
+
+    a33, b33 = t33[0], t33[1]
+    enter = unpack(tvec[0])
+    full_a33, full_b33 = blk(a33), blk(b33)
+    op_a33, op_b33 = halves(full_a33), halves(full_b33)
+    op = halves(blk(mm(op_b33, halves(a33))))
+    i3 = apply_iterate(op, mm(op_b33, halves(enter)) + unpack(tvec[1]))
+    j3 = enter + mm(op_a33, halves(i3))
+    inner = jnp.where(upper_pair, j3, i3)
+
+    @pl.when(side == 0)
+    def _():
+        goal = jnp.where(upper_pair, illum_half(observed, 1), illum_half(observed, 0))
+        misfit = mm(op_left, halves(given)) + mm(op_right, halves(inner)) - goal
+        mbuf[...] = pack(misfit)
+        vbuf[pair] = pack(mm(op_right_t, halves(misfit)))
+        for d in range(3):
+            remote(vbuf.at[pair], vbuf.at[pair], vs_sem.at[d], vr_sem.at[pair], {"box": boxes[d]}).start()
+        remote(mbuf, mbuf, ms_sem, mr_sem, {"box": mate}).start()
+
+    flip_a33, flip_b33 = full_a33.T, full_b33.T
+    op_at, op_bt = halves(flip_a33), halves(flip_b33)
+    op = halves(blk(mm(op_bt, halves(flip_a33[:, :H]))))
+
+    for s in range(2):
+
+        @pl.when(box != 2 * s)
+        def _():
+            remote(vbuf.at[s], vbuf.at[s], vs_sem.at[0], vr_sem.at[s], {"box": boxes[0]}).wait_recv()
+
+    crossed = unpack(vbuf[0])
+    l3 = apply_iterate(op, mm(op_bt, halves(crossed)) + unpack(vbuf[1]))
+    k3 = crossed + mm(op_at, halves(l3))
+
+    @pl.when(east)
+    def _():
+        remote(mbuf, mbuf, ms_sem, mr_sem, {"box": mate}).wait_recv()
+
+    back = unpack(mbuf[...])
+    below = jnp.where(upper_pair, k3, l3)
+    inner_in = mm(load_halves(inc2), halves(jnp.concatenate([given, inner], axis=0)))
+    inner_back = mm(load_halves(adj2), halves(jnp.concatenate([back, below], axis=0)))
+    in_outer = jnp.where(east, inner, given)
+    back_outer = jnp.where(east, below, back)
+    split_in = halves(jnp.concatenate([in_outer, inner_in], axis=0))
+    split_back = halves(jnp.concatenate([back_outer, inner_back], axis=0))
+
+    ones = jnp.ones((8, 32), jnp.bfloat16)
+    across = (((1,), (1,)), ((), ()))
+    for leaf in range(2):
+        outer_in = inner_in if leaf else in_outer
+        outer_back = inner_back if leaf else back_outer
+        leaf_in = mm(load_halves(inc1.at[leaf]), split_in)
+        leaf_back = mm(load_halves(adj1.at[leaf]), split_back)
+        in_re = jnp.concatenate([outer_in[:H], leaf_in[:H]], axis=0)
+        in_im = jnp.concatenate([outer_in[H:], leaf_in[H:]], axis=0)
+        back_re = jnp.concatenate([outer_back[:H], leaf_back[:H]], axis=0)
+        back_im = jnp.concatenate([outer_back[H:], leaf_back[H:]], axis=0)
+        probe_in = jnp.concatenate(
+            [jnp.concatenate([in_re, in_im], axis=1), jnp.concatenate([-in_im, in_re], axis=1)], axis=0
+        )
+        lift_in = jnp.concatenate(
+            [jnp.concatenate([back_re, -back_im], axis=1), jnp.concatenate([back_im, back_re], axis=1)], axis=0
+        )
+        lifted = mm(halves(jnp.concatenate([lbuf[leaf, 0], lbuf[leaf, 1]], axis=1)), halves(lift_in))
+        probed = mm(halves(jnp.concatenate([pbuf[leaf, 0], pbuf[leaf, 1]], axis=1)), halves(probe_in))
+        contrib = lifted[:, :32] * probed[:, :32] - lifted[:, 32:] * probed[:, 32:]
+        contrib = halves(contrib * squared)
+        summed = [lax.dot_general(ones, part, across, preferred_element_type=F32) for part in contrib]
+        summed = summed[0] + summed[1]
+        gpart[0, leaf : leaf + 1, :] = summed[0:1, :H]
+        gpart[1, leaf : leaf + 1, :] = summed[0:1, H:]
+
+    place = row * 2 + core
+    grecv[place] = gpart[row]
+    ends = []
+    for d, (r, c) in enumerate([(other, core), (row, 1 - core), (other, 1 - core)]):
+        copy = remote(gpart.at[r], grecv.at[place], gs_sem.at[d], gr_sem.at[place], peers[d])
+        copy.start()
+        sends.append(copy)
+        slot = grecv.at[r * 2 + c]
+        ends.append(remote(slot, slot, gs_sem.at[d], gr_sem.at[r * 2 + c], peers[d]))
+    for copy in ends:
+        copy.wait_recv()
+    gtot[box] = (grecv[0] + grecv[1]) + (grecv[2] + grecv[3])
+    for d in range(3):
+        copy = remote(gtot.at[box], gtot.at[box], hs_sem.at[d], hr_sem.at[box], {"box": boxes[d]})
+        copy.start()
+        sends.append(copy)
+    for d in range(3):
+        slot = gtot.at[boxes[d]]
+        remote(slot, slot, hs_sem.at[d], hr_sem.at[boxes[d]], {"box": boxes[d]}).wait_recv()
+    for j in range(2):
+        total = jnp.zeros((1, H), F32)
+        for t in range(8):
+            total = total + jnp.where(order[t] == box * 2 + j, gtot[t // 2, t % 2 : t % 2 + 1, :], 0.0)
+        out[j : j + 1, :] = total
+
+    for copy in sends:
+        copy.wait_send()
+
+    @pl.when(east)
+    def _():
+        for d in range(3):
+            where = {"box": boxes[d]}
+            remote(t33.at[pair], t33.at[pair], ts_sem.at[d], tr_sem.at[pair], where).wait_send()
+            remote(tvec.at[pair], tvec.at[pair], us_sem.at[d], ur_sem.at[pair], where).wait_send()
+
+    @pl.when(side == 0)
+    def _():
+        for d in range(3):
+            remote(vbuf.at[pair], vbuf.at[pair], vs_sem.at[d], vr_sem.at[pair], {"box": boxes[d]}).wait_send()
+        remote(mbuf, mbuf, ms_sem, mr_sem, {"box": mate}).wait_send()
+
+
+def fused(*args):
+    half = jnp.bfloat16
+    dma = pltpu.SemaphoreType.DMA
+    scratch = [
+        pltpu.VMEM((2, 2, 2 * H, 2 * H), F32),
+        pltpu.VMEM((2, 2, 2 * H, 2 * H), F32),
+        pltpu.VMEM((2, 2, 2 * H, 2 * H), F32),
+        pltpu.VMEM((4, 2, 2, H), F32),
+        pltpu.VMEM((3, 2 * H, H), F32),
+        pltpu.VMEM((3, 2 * H, H), F32),
+        pltpu.VMEM((2, 2 * H, H), F32),
+        pltpu.VMEM((2, H // 2, H), F32),
+        pltpu.VMEM((H // 2, H), F32),
+        pltpu.VMEM((2, H // 2, H), F32),
+        pltpu.VMEM((2, 2, 2 * H, 4 * H), half),
+        pltpu.VMEM((2, 2, 2 * H, 4 * H), half),
+        pltpu.VMEM((2, 2 * H, 4 * H), half),
+        pltpu.VMEM((2, 2 * H, 4 * H), half),
+        pltpu.VMEM((2, 2, H), F32),
+        pltpu.VMEM((4, 2, H), F32),
+        pltpu.VMEM((4, 2, H), F32),
+        dma((6,)), dma((9,)), dma((9,)), dma((3,)), dma((4,)), dma((3,)), dma((3,)),
+        dma((3,)), dma((2,)), dma((3,)), dma((2,)), dma(()), dma(()), dma((3,)), dma((2,)),
+        dma((3,)), dma((4,)), dma((3,)), dma((4,)),
+    ]
+    hbm, vmem, smem = [
+        pl.BlockSpec(memory_space=space) for space in (pl.ANY, pltpu.VMEM, pltpu.SMEM)
+    ]
+    return pl.pallas_call(
+        kernel,
+        out_shape=jax.ShapeDtypeStruct((2, H), F32),
+        in_specs=[hbm, hbm, hbm, smem, vmem, smem, vmem, vmem],
+        out_specs=vmem,
+        scratch_shapes=scratch,
+        compiler_params=pltpu.CompilerParams(
+            collective_id=0, has_side_effects=True, vmem_limit_bytes=48 * 2**20
+        ),
+        name="gradient",
+    )(*args)
+
+
+def pick(mesh):
+    def local(*args):
+        shape = mesh.shape
+        fits = shape["box"] == 4 and shape["row"] == 2 and shape["freq"] == 2
+        fits = fits and args[0].shape == (2, 2, 2, 256, 256) and args[6].shape == (1, 2, 2, 256, 32)
+        return (fused if fits else body)(*args)
+
+    return local
+
+
 def solution(mesh):
     return jax.shard_map(
-        body,
+        pick(mesh),
         mesh=mesh,
         in_specs=(
             P(("group", "box"), "freq", None, None, None),

time: 301 us -> 78.1 us (0.26); the launches traced: 296 us -> 77.8 us
  waiting for transfers between devices: 118 us -> 0 us
  matrix products: 110 us -> 0 us
  Pallas kernels: 0 us -> 69 us
  blocking collectives: 26.9 us -> 0 us
  between operations: 16.5 us -> 0.04 us
  other arithmetic: 11.1 us -> 0 us
  starting transfers between devices: 3.96 us -> 0 us
    dot_general x319 -> x0, matrix products: 110 us -> none  [the longest x79 27.8 us: complex_mul(): product(real_a, real_b) - product(imag_a, imag_b)]
    pallas_call x0 -> x1, Pallas kernels: none -> 69 us  [fused(): pl.pallas_call(kernel, out_shape=jax.ShapeDtypeStruct((2, H), F32), in_sp...]
    ppermute x2 -> x0, waiting for transfers between devices: 60.3 us -> none  [from_partner(): return lax.ppermute(block, axis, route)]
    psum x1 -> x0, waiting for transfers between devices: 57.7 us -> none  [body(): node_maps = base_maps + lax.psum(complex_mul(lift_swapped, weighted), 'row')]
    all_gather x1 -> x0, blocking collectives: 12.8 us -> none  [body(): every_contrast = lax.all_gather(contrast, 'box', axis=0, tiled=True)]
    unnamed x1 -> x0, blocking collectives: 11.6 us -> none
    add x18 -> x0, other arithmetic: 3.99 us -> none  [the longest x1 2.56 us: body(): node_maps = base_maps + lax.psum(complex_mul(lift_swapped, weighted), 'row')]
    ppermute x2 -> x0, starting transfers between devices: 3.96 us -> none  [from_partner(): return lax.ppermute(block, axis, route)]
  transfers between devices with their start and end apart: 3 -> 0, of which waited for: 3 -> 0; matrix products, arithmetic and copies ran while one was open for 3% -> 0% of each run, Pallas kernels for 0% -> 0%
where the time goes in v1:
time: 78.1 us; the launch traced here: 77.8 us
  Pallas kernels  69 us (88%)
  local copies, waits for them, and re-layouts  8.79 us (11%)
    pallas_call x1, Pallas kernels, fused(): pl.pallas_call(kernel, out_shape=jax.ShapeDtypeStruct((2, H), F32), in_sp...  69 us
    unnamed x15, local copies, waits for them, and re-layouts  8.79 us

profile of v1, /device:TPU:0, one launch (start us, length us, event | category | flops | bytes accessed | tf_op | source)
XLA Modules:
  0.0 77.8 jit_solution(16780555793257794885)
XLA Ops:
  0.0 1.1 %copy.9.illum = f32[1,2,2,256,32]{4,3,2,1,0:T(8,128)S(1)} copy(f32[1,2,2,256,32]{3,4,2,1,0:T(8,128)} %param.14) | data formatting | bytes 262144 | tf_op args[6]
  1.1 1.1 %copy.10.observed = f32[1,2,2,256,32]{4,3,2,1,0:T(8,128)S(1)} copy(f32[1,2,2,256,32]{3,4,2,1,0:T(8,128)} %param.15) | data formatting | bytes 262144 | tf_op args[7]
  2.2 0.0 copy-start
  2.2 1.6 %copy-done = f32[2,2,2,256,256]{4,3,2,1,0:T(8,128)S(1)} copy-done((f32[2,2,2,256,256]{4,3,2,1,0:T(8,128)S(1)}, f32[2,2,2,256,256]{4,3,2,1,0:T(8,128)}, u32[]{:S(2)}) %copy-start) | copy-done | bytes 2097176
  3.8 0.0 copy-start.1
  3.8 1.2 %copy-done.1 = f32[2,2,2,128,256]{4,3,2,1,0:T(8,128)S(1)} copy-done((f32[2,2,2,128,256]{4,3,2,1,0:T(8,128)S(1)}, f32[2,2,2,128,256]{4,3,2,1,0:T(8,128)}, u32[]{:S(2)}) %copy-start.1) | copy-done | bytes 1048600
  5.0 0.0 copy-start.2
  5.0 1.2 %copy-done.2 = f32[2,2,2,128,256]{4,3,2,1,0:T(8,128)S(1)} copy-done((f32[2,2,2,128,256]{4,3,2,1,0:T(8,128)S(1)}, f32[2,2,2,128,256]{4,3,2,1,0:T(8,128)}, u32[]{:S(2)}) %copy-start.2) | copy-done | bytes 1048600
  6.3 0.0 copy-start.3
  6.3 0.7 copy-done.3
  6.9 0.0 copy-start.4
  6.9 0.7 copy-done.4
  7.6 0.0 copy-start.5
  7.6 0.7 copy-done.5
  8.3 69.0 %gradient.1 = f32[2,128]{1,0:T(2,128)S(1)} custom-call(f32[2,2,2,256,256]{4,3,2,1,0:T(8,128)S(1)} %copy-done, f32[2,2,2,128,256]{4,3,2,1,0:T(8,128)S(1)} %copy-done.1, f32[2,2,2,128,256]{4,3,2,1,0:T(8,128)S(1)} %copy-done.2, f32[2]{0:T(128)S(1)} %copy-done.4, f32[2,128]{1,0:T(2,128)S(1)} %copy-done.3, s32[8]{0:T(128)S(1)} %copy-done.5, ...), custom_call_target="tpu_custom_call" | custom-call | tf_op jit(solution)/shard_map/gradient/pallas_call | solution.py:572
  77.2 0.6 copy.12
Async XLA Ops:
  2.2 1.6 %copy-start = (f32[2,2,2,256,256]{4,3,2,1,0:T(8,128)S(1)}, f32[2,2,2,256,256]{4,3,2,1,0:T(8,128)}, u32[]{:S(2)}) copy-start(f32[2,2,2,256,256]{4,3,2,1,0:T(8,128)} %base.1) | copy-start | bytes 6291460
  3.8 1.2 %copy-start.1 = (f32[2,2,2,128,256]{4,3,2,1,0:T(8,128)S(1)}, f32[2,2,2,128,256]{4,3,2,1,0:T(8,128)}, u32[]{:S(2)}) copy-start(f32[2,2,2,128,256]{4,3,2,1,0:T(8,128)} %lift.1) | copy-start | bytes 3145732
  5.0 1.2 %copy-start.2 = (f32[2,2,2,128,256]{4,3,2,1,0:T(8,128)S(1)}, f32[2,2,2,128,256]{4,3,2,1,0:T(8,128)}, u32[]{:S(2)}) copy-start(f32[2,2,2,128,256]{4,3,2,1,0:T(8,128)} %probe.1) | copy-start | bytes 3145732
  6.3 0.7 copy-start.3
  6.9 0.7 copy-start.4
  7.6 0.7 copy-start.5

commit v2 on v1

--- a/solution.py
+++ b/solution.py
@@ -252,7 +252,8 @@
 
 
 def kernel(
-    base, lift, probe, wave, contrast, order, illum, observed, out,
+    base, lift, probe, wave_in, contrast, order_in, illum_in, observed_in, out,
+    wave, order, illum, observed, opl, opr, oprt, evec, gvec, es_sem, er_sem,
     lbuf, pbuf, bbuf, cbuf, own, got, t33, tvec, mbuf, vbuf, inc1, adj1, inc2, adj2,
     gpart, grecv, gtot, loc_sem, xs_sem, xr_sem, cs_sem, cr_sem, zs_sem, zr_sem,
     ts_sem, tr_sem, us_sem, ur_sem, ms_sem, mr_sem, vs_sem, vr_sem, gs_sem, gr_sem, hs_sem, hr_sem,
@@ -282,6 +283,8 @@
             (probe.at[leaf, row], pbuf.at[leaf, :, mine, :]),
             (base.at[leaf, row], bbuf.at[leaf]),
         ]
+    loads += [(wave_in, wave), (order_in, order), (illum_in.at[0, row], illum)]
+    loads += [(observed_in.at[0, row], observed), (contrast, cbuf.at[box, row])]
     loads = [pltpu.make_async_copy(s, t, loc_sem.at[i]) for i, (s, t) in enumerate(loads)]
     for load in loads:
         load.start()
@@ -291,13 +294,12 @@
         pl.semaphore_signal(barrier, inc=1, device_id=where, device_id_type=MESH)
     pl.semaphore_wait(barrier, 6)
 
-    cbuf[box, row] = contrast[...]
-    ahead = remote(contrast, cbuf.at[box, row], xs_sem.at[8], xr_sem.at[8], peers[0])
-    ahead.start()
+    early = remote(contrast, cbuf.at[box, row], xs_sem.at[8], xr_sem.at[8], peers[0])
+    early.start()
     low, high = pl.ds(0, H), pl.ds(H, H)
     plan = [(lift, lbuf, 0, high), (probe, pbuf, 0, high), (lift, lbuf, 1, high), (probe, pbuf, 1, high)]
     plan += [(probe, pbuf, 0, low), (probe, pbuf, 1, low), (lift, lbuf, 0, low), (lift, lbuf, 1, low)]
-    sends, waits = [ahead], []
+    sends, waits = [early], []
     for i, (source, target, leaf, cols) in enumerate(plan):
         copy = remote(
             source.at[leaf, other, :, :, cols], target.at[leaf, :, mine, cols],
@@ -312,6 +314,8 @@
             )
         )
 
+    for load in loads:
+        load.wait()
     remote(contrast, cbuf.at[box, other], xs_sem.at[8], xr_sem.at[8], peers[0]).wait_recv()
     for d in range(3):
         copy = remote(cbuf.at[box], cbuf.at[box], cs_sem.at[d], cr_sem.at[box], {"box": boxes[d]})
@@ -333,8 +337,6 @@
             jnp.concatenate([jnp.broadcast_to(total[i : i + 1], (H, H)).T for i in range(2)], axis=0)
         )
 
-    for load in loads:
-        load.wait()
     for copy in waits[:4]:
         copy.wait_recv()
 
@@ -372,52 +374,90 @@
     own[0] = low_right
     own[1] = low_left
     own[2] = top_right
-    for i in range(3):
-        copy = remote(own.at[i], got.at[i], zs_sem.at[i], zr_sem.at[i], {"box": mate})
-        copy.start()
-        sends.append(copy)
+    def illum_half(ref, part):
+        rows = pl.ds(part * H, H)
+        return jnp.concatenate([ref[0, :, rows].T, ref[1, :, rows].T], axis=0)
+
+    i1, j2 = illum_half(illum, 0), illum_half(illum, 1)
+    upper_pair = pair == 1
+    east = side == 1
+    given = jnp.where(upper_pair, j2, i1)
+
+    swaps = [remote(own.at[i], got.at[i], zs_sem.at[i], zr_sem.at[i], {"box": mate}) for i in range(3)]
+    ahead = remote(evec, gvec, es_sem, er_sem, {"box": mate})
+    sends += swaps
+    swaps[0].start()
+
+    @pl.when(side == 0)
+    def _():
+        evec[...] = pack(mm(halves(blk(low_left)), halves(given)))
+        ahead.start()
+
+    @pl.when(east)
+    def _():
+        swaps[1].start()
+
     store_halves(inc1.at[0], wide(reach))
     store_halves(inc1.at[1], wide(echo))
     to_l3, to_k3 = adjoint_maps(a13, a33, b23, b33)
     store_halves(adj1.at[0], to_l3)
     store_halves(adj1.at[1], to_k3)
 
-    def illum_half(ref, part):
-        rows = pl.ds(part * H, H)
-        return jnp.concatenate([ref[0, row, 0, rows, :], ref[0, row, 1, rows, :]], axis=0)
-
-    i1, j2 = illum_half(illum, 0), illum_half(illum, 1)
-    upper_pair = pair == 1
-    east = side == 1
-    given = jnp.where(upper_pair, j2, i1)
-
-    for i in range(2):
-        remote(own.at[i], got.at[i], zs_sem.at[i], zr_sem.at[i], {"box": mate}).wait_recv()
+    @pl.when(side == 0)
+    def _():
+        swaps[1].start()
+
+    swaps[2].start()
+
+    swaps[0].wait_recv()
     a33, b33 = jnp.where(east, got[0], low_right), jnp.where(east, low_right, got[0])
-    a31, b32 = jnp.where(east, got[1], low_left), jnp.where(east, low_left, got[1])
     op_a33, op_b33 = halves(blk(a33)), halves(blk(b33))
     op = halves(blk(mm(op_b33, halves(a33))))
+    far, mid, first = {"box": 4 - box}, {"box": 2}, {"box": 0}
+    tops = []
+    for i, (where, slot) in enumerate([(far, pair), (mid, pair), (first, 0), (first, 1)]):
+        tops.append(
+            [
+                remote(t33.at[slot], t33.at[slot], ts_sem.at[i], tr_sem.at[slot], where),
+                remote(tvec.at[slot], tvec.at[slot], us_sem.at[i], ur_sem.at[slot], where),
+            ]
+        )
+
+    @pl.when(east)
+    def _():
+        ahead.wait_recv()
+        enter = unpack(gvec[...])
+        seen = jnp.concatenate([low_left, mm(op_b33, halves(enter))], axis=1)
+        seen = mm(op_a33, halves(apply_iterate(op, seen)))
+        seen = jnp.concatenate([seen[:, :H], seen[:, H:] + enter], axis=1)
+        seen = mm(halves(blk(top_right)), halves(seen))
+        t33[pair] = seen[:, :H] + top_left
+        tvec[pair] = pack(seen[:, H:])
+        for copy in tops[0] + tops[1]:
+            copy.start()
+
+    @pl.when(box == 1)
+    def _():
+        for copy in tops[2]:
+            copy.start()
+
+    swaps[1].wait_recv()
+    a31, b32 = jnp.where(east, got[1], low_left), jnp.where(east, low_left, got[1])
     reach, echo = incoming_maps(op_a33, op, mm(op_b33, halves(a31)), a31, b32)
-    half_map = mm(halves(blk(top_right)), halves(jnp.where(east, echo, reach)))
-    left = half_map[:, :H] + jnp.where(east, 0.0, top_left)
-    right = half_map[:, H:] + jnp.where(east, top_left, 0.0)
-    op_left, op_right = halves(blk(left)), halves(blk(right))
-
-    @pl.when(east)
-    def _():
-        t33[pair] = right
-        tvec[pair] = pack(mm(op_left, halves(given)))
-        for d in range(3):
-            where = {"box": boxes[d]}
-            remote(t33.at[pair], t33.at[pair], ts_sem.at[d], tr_sem.at[pair], where).start()
-            remote(tvec.at[pair], tvec.at[pair], us_sem.at[d], ur_sem.at[pair], where).start()
+
+    @pl.when(side == 0)
+    def _():
+        half_map = mm(halves(blk(top_right)), halves(reach))
+        right = blk(half_map[:, H:])
+        store_halves(opl, blk(half_map[:, :H] + top_left))
+        store_halves(opr, right)
+        store_halves(oprt, right.T)
 
     store_halves(inc2, wide(jnp.where(east, echo, reach)))
-    remote(own.at[2], got.at[2], zs_sem.at[2], zr_sem.at[2], {"box": mate}).wait_recv()
+    swaps[2].wait_recv()
     a13, b23 = jnp.where(east, got[2], top_right), jnp.where(east, top_right, got[2])
     to_l3, to_k3 = adjoint_maps(a13, a33, b23, b33)
     store_halves(adj2, jnp.where(east, to_k3, to_l3))
-    op_right_t = halves(blk(right).T)
 
     for s in range(2):
 
@@ -426,6 +466,11 @@
             where = {"box": boxes[0]}
             remote(t33.at[s], t33.at[s], ts_sem.at[0], tr_sem.at[s], where).wait_recv()
             remote(tvec.at[s], tvec.at[s], us_sem.at[0], ur_sem.at[s], where).wait_recv()
+
+    @pl.when(box == 1)
+    def _():
+        for copy in tops[3]:
+            copy.start()
 
     a33, b33 = t33[0], t33[1]
     enter = unpack(tvec[0])
@@ -439,9 +484,9 @@
     @pl.when(side == 0)
     def _():
         goal = jnp.where(upper_pair, illum_half(observed, 1), illum_half(observed, 0))
-        misfit = mm(op_left, halves(given)) + mm(op_right, halves(inner)) - goal
+        misfit = mm(load_halves(opl), halves(given)) + mm(load_halves(opr), halves(inner)) - goal
         mbuf[...] = pack(misfit)
-        vbuf[pair] = pack(mm(op_right_t, halves(misfit)))
+        vbuf[pair] = pack(mm(load_halves(oprt), halves(misfit)))
         for d in range(3):
             remote(vbuf.at[pair], vbuf.at[pair], vs_sem.at[d], vr_sem.at[pair], {"box": boxes[d]}).start()
         remote(mbuf, mbuf, ms_sem, mr_sem, {"box": mate}).start()
@@ -529,22 +574,37 @@
 
     @pl.when(east)
     def _():
-        for d in range(3):
-            where = {"box": boxes[d]}
-            remote(t33.at[pair], t33.at[pair], ts_sem.at[d], tr_sem.at[pair], where).wait_send()
-            remote(tvec.at[pair], tvec.at[pair], us_sem.at[d], ur_sem.at[pair], where).wait_send()
+        for copy in tops[0] + tops[1]:
+            copy.wait_send()
+
+    @pl.when(box == 1)
+    def _():
+        for copy in tops[2] + tops[3]:
+            copy.wait_send()
 
     @pl.when(side == 0)
     def _():
         for d in range(3):
             remote(vbuf.at[pair], vbuf.at[pair], vs_sem.at[d], vr_sem.at[pair], {"box": boxes[d]}).wait_send()
         remote(mbuf, mbuf, ms_sem, mr_sem, {"box": mate}).wait_send()
+        ahead.wait_send()
 
 
 def fused(*args):
     half = jnp.bfloat16
     dma = pltpu.SemaphoreType.DMA
     scratch = [
+        pltpu.SMEM((2,), F32),
+        pltpu.SMEM((8,), jnp.int32),
+        pltpu.VMEM((2, 32, 2 * H), F32),
+        pltpu.VMEM((2, 32, 2 * H), F32),
+        pltpu.VMEM((2, 2 * H, 2 * H), half),
+        pltpu.VMEM((2, 2 * H, 2 * H), half),
+        pltpu.VMEM((2, 2 * H, 2 * H), half),
+        pltpu.VMEM((H // 2, H), F32),
+        pltpu.VMEM((H // 2, H), F32),
+        dma(()),
+        dma(()),
         pltpu.VMEM((2, 2, 2 * H, 2 * H), F32),
         pltpu.VMEM((2, 2, 2 * H, 2 * H), F32),
         pltpu.VMEM((2, 2, 2 * H, 2 * H), F32),
@@ -562,24 +622,22 @@
         pltpu.VMEM((2, 2, H), F32),
         pltpu.VMEM((4, 2, H), F32),
         pltpu.VMEM((4, 2, H), F32),
-        dma((6,)), dma((9,)), dma((9,)), dma((3,)), dma((4,)), dma((3,)), dma((3,)),
-        dma((3,)), dma((2,)), dma((3,)), dma((2,)), dma(()), dma(()), dma((3,)), dma((2,)),
+        dma((11,)), dma((9,)), dma((9,)), dma((3,)), dma((4,)), dma((3,)), dma((3,)),
+        dma((4,)), dma((2,)), dma((4,)), dma((2,)), dma(()), dma(()), dma((3,)), dma((2,)),
         dma((3,)), dma((4,)), dma((3,)), dma((4,)),
     ]
-    hbm, vmem, smem = [
-        pl.BlockSpec(memory_space=space) for space in (pl.ANY, pltpu.VMEM, pltpu.SMEM)
-    ]
+    hbm, vmem = [pl.BlockSpec(memory_space=space) for space in (pltpu.HBM, pltpu.VMEM)]
     return pl.pallas_call(
         kernel,
         out_shape=jax.ShapeDtypeStruct((2, H), F32),
-        in_specs=[hbm, hbm, hbm, smem, vmem, smem, vmem, vmem],
+        in_specs=[hbm] * 8,
         out_specs=vmem,
         scratch_shapes=scratch,
         compiler_params=pltpu.CompilerParams(
-            collective_id=0, has_side_effects=True, vmem_limit_bytes=48 * 2**20
+            collective_id=0, has_side_effects=True, vmem_limit_bytes=63 * 2**20
         ),
         name="gradient",
-    )(*args)
+    )(*args[:6], *[jnp.swapaxes(x, -1, -2) for x in args[6:]])
 
 
 def pick(mesh):

time: 78.1 us -> 69.9 us (0.90)
  local copies, waits for them, and re-layouts: 8.79 us -> 1.24 us
    unnamed x15 -> x1, local copies, waits for them, and re-layouts: 8.79 us -> 1.24 us
where the time goes in v2:
time: 69.9 us; the launch traced here: 69.8 us
  Pallas kernels  68.5 us (98%)
  local copies, waits for them, and re-layouts  1.24 us (2%)
    pallas_call x1, Pallas kernels, fused(): pl.pallas_call(kernel, out_shape=jax.ShapeDtypeStruct((2, H), F32), in_sp...  68.5 us

profile of v2, /device:TPU:0, one launch (start us, length us, event | category | flops | bytes accessed | tf_op | source)
XLA Modules:
  0.0 69.8 jit_solution(7821911605888018917)
XLA Ops:
  0.0 68.5 %gradient.1 = f32[2,128]{1,0:T(2,128)} custom-call(f32[2,2,2,256,256]{4,3,2,1,0:T(8,128)} %base.1, f32[2,2,2,128,256]{4,3,2,1,0:T(8,128)} %lift.1, f32[2,2,2,128,256]{4,3,2,1,0:T(8,128)} %probe.1, f32[2]{0:T(128)} %wave_in.1, f32[2,128]{1,0:T(2,128)} %contrast.1, s32[8]{0:T(128)} %order_in.1, f32[1,2,2,32,256]{4,3,2,1,0:T(8,128)} %bitcast.2, ...), custom_call_target="tpu_custom_call" | custom-call | tf_op jit(solution)/shard_map/gradient/pallas_call | solution.py:630
  68.5 1.2 %copy.10 = f32[2,128]{1,0:T(2,128)} copy(f32[2,128]{1,0:T(2,128)} %gradient.1) | data formatting | bytes 2048

commit v3 on v2

--- a/solution.py
+++ b/solution.py
@@ -255,8 +255,8 @@
     base, lift, probe, wave_in, contrast, order_in, illum_in, observed_in, out,
     wave, order, illum, observed, opl, opr, oprt, evec, gvec, es_sem, er_sem,
     lbuf, pbuf, bbuf, cbuf, own, got, t33, tvec, mbuf, vbuf, inc1, adj1, inc2, adj2,
-    gpart, grecv, gtot, loc_sem, xs_sem, xr_sem, cs_sem, cr_sem, zs_sem, zr_sem,
-    ts_sem, tr_sem, us_sem, ur_sem, ms_sem, mr_sem, vs_sem, vr_sem, gs_sem, gr_sem, hs_sem, hr_sem,
+    gpart, grecv, loc_sem, xs_sem, xr_sem, cs_sem, cr_sem, zs_sem, zr_sem,
+    ts_sem, tr_sem, us_sem, ur_sem, ms_sem, mr_sem, vs_sem, vr_sem, gs_sem, gr_sem,
 ):
     box = lax.axis_index("box")
     row = lax.axis_index("row")
@@ -290,9 +290,16 @@
         load.start()
 
     barrier = pltpu.get_barrier_semaphore()
-    for where in peers + [{"box": b} for b in boxes]:
+    others = []
+    for d in (2, 1, 3, 0):
+        for i in range(2):
+            for j in range(2):
+                if d + i + j > 0:
+                    place = lax.rem(box + d, 4), lax.rem(row + i, 2), lax.rem(core + j, 2)
+                    others.append(dict(zip(("box", "row", "freq"), place)))
+    for where in others:
         pl.semaphore_signal(barrier, inc=1, device_id=where, device_id_type=MESH)
-    pl.semaphore_wait(barrier, 6)
+    pl.semaphore_wait(barrier, 15)
 
     early = remote(contrast, cbuf.at[box, row], xs_sem.at[8], xr_sem.at[8], peers[0])
     early.start()
@@ -433,7 +440,7 @@
         seen = mm(halves(blk(top_right)), halves(seen))
         t33[pair] = seen[:, :H] + top_left
         tvec[pair] = pack(seen[:, H:])
-        for copy in tops[0] + tops[1]:
+        for copy in tops[0]:
             copy.start()
 
     @pl.when(box == 1)
@@ -444,6 +451,11 @@
     swaps[1].wait_recv()
     a31, b32 = jnp.where(east, got[1], low_left), jnp.where(east, low_left, got[1])
     reach, echo = incoming_maps(op_a33, op, mm(op_b33, halves(a31)), a31, b32)
+
+    @pl.when(east)
+    def _():
+        for copy in tops[1]:
+            copy.start()
 
     @pl.when(side == 0)
     def _():
@@ -544,29 +556,24 @@
         gpart[0, leaf : leaf + 1, :] = summed[0:1, :H]
         gpart[1, leaf : leaf + 1, :] = summed[0:1, H:]
 
-    place = row * 2 + core
+    place = box * 4 + row * 2 + core
     grecv[place] = gpart[row]
     ends = []
-    for d, (r, c) in enumerate([(other, core), (row, 1 - core), (other, 1 - core)]):
-        copy = remote(gpart.at[r], grecv.at[place], gs_sem.at[d], gr_sem.at[place], peers[d])
+    for i, where in enumerate(others):
+        copy = remote(gpart.at[where["row"]], grecv.at[place], gs_sem.at[i], gr_sem.at[place], where)
         copy.start()
         sends.append(copy)
-        slot = grecv.at[r * 2 + c]
-        ends.append(remote(slot, slot, gs_sem.at[d], gr_sem.at[r * 2 + c], peers[d]))
+        source = where["box"] * 4 + where["row"] * 2 + where["freq"]
+        ends.append(remote(grecv.at[source], grecv.at[source], gs_sem.at[i], gr_sem.at[source], where))
     for copy in ends:
         copy.wait_recv()
-    gtot[box] = (grecv[0] + grecv[1]) + (grecv[2] + grecv[3])
-    for d in range(3):
-        copy = remote(gtot.at[box], gtot.at[box], hs_sem.at[d], hr_sem.at[box], {"box": boxes[d]})
-        copy.start()
-        sends.append(copy)
-    for d in range(3):
-        slot = gtot.at[boxes[d]]
-        remote(slot, slot, hs_sem.at[d], hr_sem.at[boxes[d]], {"box": boxes[d]}).wait_recv()
+    sums = []
+    for b in range(4):
+        sums.append((grecv[4 * b] + grecv[4 * b + 1]) + (grecv[4 * b + 2] + grecv[4 * b + 3]))
     for j in range(2):
         total = jnp.zeros((1, H), F32)
         for t in range(8):
-            total = total + jnp.where(order[t] == box * 2 + j, gtot[t // 2, t % 2 : t % 2 + 1, :], 0.0)
+            total = total + jnp.where(order[t] == box * 2 + j, sums[t // 2][t % 2 : t % 2 + 1, :], 0.0)
         out[j : j + 1, :] = total
 
     for copy in sends:
@@ -620,11 +627,10 @@
         pltpu.VMEM((2, 2 * H, 4 * H), half),
         pltpu.VMEM((2, 2 * H, 4 * H), half),
         pltpu.VMEM((2, 2, H), F32),
-        pltpu.VMEM((4, 2, H), F32),
-        pltpu.VMEM((4, 2, H), F32),
+        pltpu.VMEM((16, 2, H), F32),
         dma((11,)), dma((9,)), dma((9,)), dma((3,)), dma((4,)), dma((3,)), dma((3,)),
         dma((4,)), dma((2,)), dma((4,)), dma((2,)), dma(()), dma(()), dma((3,)), dma((2,)),
-        dma((3,)), dma((4,)), dma((3,)), dma((4,)),
+        dma((15,)), dma((16,)),
     ]
     hbm, vmem = [pl.BlockSpec(memory_space=space) for space in (pltpu.HBM, pltpu.VMEM)]
     return pl.pallas_call(

time: 69.9 us -> 68.2 us (0.976)
  Pallas kernels: 68.5 us -> 66.9 us
    pallas_call x1, Pallas kernels: 68.5 us -> 66.9 us  [fused(): pl.pallas_call(kernel, out_shape=jax.ShapeDtypeStruct((2, H), F32), in_sp...]
where the time goes in v3:
time: 68.2 us; the launch traced here: 68.1 us
  Pallas kernels  66.9 us (98%)
  local copies, waits for them, and re-layouts  1.24 us (2%)
    pallas_call x1, Pallas kernels, fused(): pl.pallas_call(kernel, out_shape=jax.ShapeDtypeStruct((2, H), F32), in_sp...  66.9 us

profile of v3, /device:TPU:0, one launch (start us, length us, event | category | flops | bytes accessed | tf_op | source)
XLA Modules:
  0.0 68.1 jit_solution(6614706664584166019)
XLA Ops:
  0.0 66.9 %gradient.1 = f32[2,128]{1,0:T(2,128)} custom-call(f32[2,2,2,256,256]{4,3,2,1,0:T(8,128)} %base.1, f32[2,2,2,128,256]{4,3,2,1,0:T(8,128)} %lift.1, f32[2,2,2,128,256]{4,3,2,1,0:T(8,128)} %probe.1, f32[2]{0:T(128)} %wave_in.1, f32[2,128]{1,0:T(2,128)} %contrast.1, s32[8]{0:T(128)} %order_in.1, f32[1,2,2,32,256]{4,3,2,1,0:T(8,128)} %bitcast.2, ...), custom_call_target="tpu_custom_call" | custom-call | tf_op jit(solution)/shard_map/gradient/pallas_call | solution.py:636
  66.9 1.2 %copy.10 = f32[2,128]{1,0:T(2,128)} copy(f32[2,128]{1,0:T(2,128)} %gradient.1) | data formatting | bytes 2048

commit v4 on v3

--- a/solution.py
+++ b/solution.py
@@ -465,6 +465,12 @@
         store_halves(opr, right)
         store_halves(oprt, right.T)
 
+    @pl.when(box == 1)
+    def _():
+        for copy in tops[3]:
+            copy.wait_recv()
+            copy.start()
+
     store_halves(inc2, wide(jnp.where(east, echo, reach)))
     swaps[2].wait_recv()
     a13, b23 = jnp.where(east, got[2], top_right), jnp.where(east, top_right, got[2])
@@ -473,16 +479,11 @@
 
     for s in range(2):
 
-        @pl.when(box != 2 * s + 1)
+        @pl.when(side == 0 if s else box != 1)
         def _():
             where = {"box": boxes[0]}
             remote(t33.at[s], t33.at[s], ts_sem.at[0], tr_sem.at[s], where).wait_recv()
             remote(tvec.at[s], tvec.at[s], us_sem.at[0], ur_sem.at[s], where).wait_recv()
-
-    @pl.when(box == 1)
-    def _():
-        for copy in tops[3]:
-            copy.start()
 
     a33, b33 = t33[0], t33[1]
     enter = unpack(tvec[0])

time: 68.2 us -> 67.6 us (level)
  Pallas kernels: 66.9 us -> 66.2 us
    pallas_call x1, Pallas kernels: 66.9 us -> 66.2 us  [fused(): pl.pallas_call(kernel, out_shape=jax.ShapeDtypeStruct((2, H), F32), in_sp...]
where the time goes in v4:
time: 67.6 us; the launch traced here: 67.4 us
  Pallas kernels  66.2 us (98%)
  local copies, waits for them, and re-layouts  1.24 us (2%)
    pallas_call x1, Pallas kernels, fused(): pl.pallas_call(kernel, out_shape=jax.ShapeDtypeStruct((2, H), F32), in_sp...  66.2 us

profile of v4, /device:TPU:0, one launch (start us, length us, event | category | flops | bytes accessed | tf_op | source)
XLA Modules:
  0.0 67.4 jit_solution(16160616180129688360)
XLA Ops:
  0.0 66.2 %gradient.1 = f32[2,128]{1,0:T(2,128)} custom-call(f32[2,2,2,256,256]{4,3,2,1,0:T(8,128)} %base.1, f32[2,2,2,128,256]{4,3,2,1,0:T(8,128)} %lift.1, f32[2,2,2,128,256]{4,3,2,1,0:T(8,128)} %probe.1, f32[2]{0:T(128)} %wave_in.1, f32[2,128]{1,0:T(2,128)} %contrast.1, s32[8]{0:T(128)} %order_in.1, f32[1,2,2,32,256]{4,3,2,1,0:T(8,128)} %bitcast.2, ...), custom_call_target="tpu_custom_call" | custom-call | tf_op jit(solution)/shard_map/gradient/pallas_call | solution.py:637
  66.2 1.2 %copy.10 = f32[2,128]{1,0:T(2,128)} copy(f32[2,128]{1,0:T(2,128)} %gradient.1) | data formatting | bytes 2048
